TPU v7x, 32 devices: a whole 2x2x4 slice. The times are simulated.
32 devices in a mesh: dp: 16 (over z, y, x), head: 2 (over core).
Axes of the slice: x: 2, y: 2, z: 4, core: 2. Of those that a mesh axis runs over, the one named last changes fastest.
Arguments:
- tokens: bfloat16 [32768, 768], P(('dp', 'head')), may hold values from -6 to 6
- w_qkv: bfloat16 [768, 2304], replicated, may hold values from -0.21875 to 0.21875
- b_query: float32 [768], replicated, may hold values from -3 to 3
- b_value: float32 [768], replicated, may hold values from -0.3 to 0.3
- w_out: bfloat16 [768, 768], replicated, may hold values from -2.5 to 2.5
- b_out: float32 [768], replicated, may hold values from -2 to 2
- gain_attn: float32 [768], replicated, may hold values from 0.5 to 1.5
- shift_attn: float32 [768], replicated, may hold values from -2 to 2
- w_in: bfloat16 [768, 3072], replicated, may hold values from -0.21875 to 0.21875
- b_in: float32 [3072], replicated, may hold values from -2 to 2
- w_back: bfloat16 [3072, 768], replicated, may hold values from -0.109375 to 0.109375
- b_back: float32 [768], replicated, may hold values from -2 to 2
- gain_out: float32 [768], replicated, may hold values from 0.5 to 1.5
- shift_out: float32 [768], replicated, may hold values from -2 to 2
- grad_out: bfloat16 [32768, 768], P(('dp', 'head')), may hold values from -6 to 6
- masked: int32 [32768], P(('dp', 'head')), may hold values from 0 to 1, as said below
Outputs:
- layer_out: bfloat16 [32768, 768], P(('dp', 'head'))
- grad_tokens: float32 [32768, 768], P(('dp', 'head'))
- grad_w_qkv: float32 [768, 2304], P('dp', 'head')
- grad_b_query: float32 [768], replicated
- grad_b_value: float32 [768], replicated
- grad_w_out: float32 [768, 768], P('dp', 'head')
- grad_b_out: float32 [768], replicated
- grad_gain_attn: float32 [768], replicated
- grad_shift_attn: float32 [768], replicated
- grad_w_in: float32 [768, 3072], P('dp', 'head')
- grad_b_in: float32 [3072], replicated
- grad_w_back: float32 [3072, 768], P('dp', 'head')
- grad_b_back: float32 [768], replicated
- grad_gain_out: float32 [768], replicated
- grad_shift_out: float32 [768], replicated
Inputs may be any that keep to these rules, and one draw needn't show every extreme that they name: `masked`: among the 1024 tokens of one device (aligned blocks of rows) at most 320 are marked and at least one; in every draw some device has exactly 320.
All inputs are finite; a program needn't handle non-finite values.
Results may differ from a plain program's by a relative error of at most 0.015.
Values may be sent and summed in bfloat16 or wider, within the bound.
No kernel may reach another device: no remote copies, remote signals or barrier semaphores. Data moves between devices by JAX's collectives and lax.ppermute only.
A program may use at most 192 MiB of HBM per device.

v0:
```python
import jax
import jax.numpy as jnp
from jax import lax
from jax.sharding import PartitionSpec as P

HEADS = 12
HEAD_DIM = 64
LEN = 512


epsilon = 1e-12


def norm_rows(values, gain, shift):
    mean = jnp.mean(values, axis=-1, keepdims=True)
    centred = values - mean
    variance = jnp.mean(centred * centred, axis=-1, keepdims=True)
    return centred * lax.rsqrt(variance + epsilon) * gain + shift


def gelu_exact(values):
    return jax.nn.gelu(values, approximate=False)


def forward(
    tokens, w_qkv, b_query, b_value, w_out, b_out, gain_attn, shift_attn, w_in, b_in, w_back, b_back
):
    rows, width = tokens.shape
    halves = lax.axis_size("head")
    local_heads = HEADS // halves
    scale = HEAD_DIM ** (-0.5)
    bias = jnp.concatenate([b_query, jnp.zeros_like(b_query), b_value])
    projected = (jnp.dot(tokens, w_qkv, preferred_element_type=jnp.float32) + bias).astype(
        jnp.bfloat16
    )
    projected = projected.reshape(rows, 3, halves, width // halves)
    by_heads = lax.all_to_all(projected, "head", split_axis=2, concat_axis=0, tiled=True)
    sequences = rows * halves // LEN
    by_heads = by_heads.reshape(sequences, LEN, 3, local_heads, HEAD_DIM)
    query = by_heads[:, :, 0]
    key_rows = by_heads[:, :, 1]
    value = by_heads[:, :, 2]
    scores = (
        jnp.einsum("sqhd,skhd->shqk", query, key_rows, preferred_element_type=jnp.float32) * scale
    )
    maxima = jnp.max(scores, axis=-1, keepdims=True)
    expo = jnp.exp(scores - maxima)
    totals = jnp.sum(expo, axis=-1, keepdims=True)
    probs = (expo / totals).astype(jnp.bfloat16)
    log_total = maxima + jnp.log(totals)
    context = jnp.einsum(
        "shqk,skhd->sqhd", probs, value, preferred_element_type=jnp.float32
    ).astype(jnp.bfloat16)
    context = context.reshape(rows * halves, 1, width // halves)
    context = lax.all_to_all(context, "head", split_axis=0, concat_axis=1, tiled=True).reshape(
        rows, width
    )
    attn = jnp.dot(context, w_out, preferred_element_type=jnp.float32) + b_out
    pre_attn = tokens.astype(jnp.float32) + attn
    hidden = norm_rows(pre_attn, gain_attn, shift_attn)
    hidden_low = hidden.astype(jnp.bfloat16)
    inner = jnp.dot(hidden_low, w_in, preferred_element_type=jnp.float32) + b_in
    active = gelu_exact(inner).astype(jnp.bfloat16)
    branch = jnp.dot(active, w_back, preferred_element_type=jnp.float32) + b_back
    return (
        query,
        key_rows,
        value,
        log_total,
        context,
        pre_attn,
        hidden,
        hidden_low,
        inner,
        active,
        branch,
    )


def dense_backward(
    cotangent,
    pre_out,
    active,
    inner,
    hidden_low,
    pre_attn,
    context,
    gain_out,
    shift_out,
    gain_attn,
    shift_attn,
    w_in,
    w_back,
    w_out,
):
    unused, out_pull = jax.vjp(norm_rows, pre_out, gain_out, shift_out)
    back_sum, back_gain_out, back_shift_out = out_pull(cotangent)
    back_branch = back_sum.astype(jnp.bfloat16)
    sum_back_bias = jnp.sum(back_branch, axis=0, dtype=jnp.float32)
    grad_w_back = jnp.einsum("rf,rd->fd", active, back_branch, preferred_element_type=jnp.float32)
    back_active = jnp.einsum("rd,fd->rf", back_branch, w_back, preferred_element_type=jnp.float32)
    unused, gelu_pull = jax.vjp(gelu_exact, inner)
    back_inner = gelu_pull(back_active)[0].astype(jnp.bfloat16)
    sum_in_bias = jnp.sum(back_inner, axis=0, dtype=jnp.float32)
    grad_w_in = jnp.einsum("rd,rf->df", hidden_low, back_inner, preferred_element_type=jnp.float32)
    back_hidden = back_sum + jnp.einsum(
        "rf,df->rd", back_inner, w_in, preferred_element_type=jnp.float32
    )
    unused, attn_pull = jax.vjp(norm_rows, pre_attn, gain_attn, shift_attn)
    back_pre, back_gain_attn, back_shift_attn = attn_pull(back_hidden)
    back_attn = back_pre.astype(jnp.bfloat16)
    sum_out_bias = jnp.sum(back_attn, axis=0, dtype=jnp.float32)
    grad_w_out = jnp.einsum("rk,rd->kd", context, back_attn, preferred_element_type=jnp.float32)
    back_context = jnp.einsum(
        "rd,kd->rk", back_attn, w_out, preferred_element_type=jnp.float32
    ).astype(jnp.bfloat16)
    return (
        back_pre,
        back_context,
        grad_w_back,
        grad_w_in,
        grad_w_out,
        sum_back_bias,
        sum_in_bias,
        sum_out_bias,
        back_gain_out,
        back_shift_out,
        back_gain_attn,
        back_shift_attn,
    )


def body(
    tokens,
    w_qkv,
    b_query,
    b_value,
    w_out,
    b_out,
    gain_attn,
    shift_attn,
    w_in,
    b_in,
    w_back,
    b_back,
    gain_out,
    shift_out,
    grad_out,
    masked,
):
    rows, width = tokens.shape
    halves = lax.axis_size("head")
    scale = HEAD_DIM ** (-0.5)
    weights = (
        w_qkv,
        b_query,
        b_value,
        w_out,
        b_out,
        gain_attn,
        shift_attn,
        w_in,
        b_in,
        w_back,
        b_back,
    )
    state = forward(tokens, *weights)
    layer_out = norm_rows(state[6] + state[10], gain_out, shift_out).astype(jnp.bfloat16)
    state = forward(tokens, *weights)
    (
        query,
        key_rows,
        value,
        log_total,
        context,
        pre_attn,
        hidden,
        hidden_low,
        inner,
        active,
        branch,
    ) = state
    cotangent = grad_out.astype(jnp.float32) * masked.astype(jnp.float32)[:, None]
    whole = dense_backward(
        cotangent,
        hidden + branch,
        active,
        inner,
        hidden_low,
        pre_attn,
        context,
        gain_out,
        shift_out,
        gain_attn,
        shift_attn,
        w_in,
        w_back,
        w_out,
    )
    back_pre, back_context = (whole[0], whole[1])
    back_context = back_context.reshape(rows, halves, width // halves)
    back_heads = lax.all_to_all(
        back_context, "head", split_axis=1, concat_axis=0, tiled=True
    ).reshape(query.shape)
    rest = whole[2:]
    (
        grad_w_back,
        grad_w_in,
        grad_w_out,
        sum_back_bias,
        sum_in_bias,
        sum_out_bias,
        back_gain_out,
        back_shift_out,
        back_gain_attn,
        back_shift_attn,
    ) = rest
    scores = (
        jnp.einsum("sqhd,skhd->shqk", query, key_rows, preferred_element_type=jnp.float32) * scale
    )
    probs_full = jnp.exp(scores - log_total)
    probs = probs_full.astype(jnp.bfloat16)
    back_value = jnp.einsum(
        "shqk,sqhd->skhd", probs, back_heads, preferred_element_type=jnp.float32
    ).astype(jnp.bfloat16)
    back_probs = jnp.einsum(
        "sqhd,skhd->shqk", back_heads, value, preferred_element_type=jnp.float32
    )
    row_terms = jnp.sum(probs_full * back_probs, axis=-1, keepdims=True)
    back_scores = (probs_full * (back_probs - row_terms)).astype(jnp.bfloat16)
    back_query = (
        jnp.einsum("shqk,skhd->sqhd", back_scores, key_rows, preferred_element_type=jnp.float32)
        * scale
    ).astype(jnp.bfloat16)
    back_key = (
        jnp.einsum("shqk,sqhd->skhd", back_scores, query, preferred_element_type=jnp.float32)
        * scale
    ).astype(jnp.bfloat16)
    stacked = jnp.stack([back_query, back_key, back_value], axis=2).reshape(
        rows * halves, 3, 1, width // halves
    )
    back_qkv = lax.all_to_all(stacked, "head", split_axis=0, concat_axis=2, tiled=True).reshape(
        rows, 3 * width
    )
    grad_w_qkv = jnp.einsum("rd,rc->dc", tokens, back_qkv, preferred_element_type=jnp.float32)
    column_sums = jnp.sum(back_qkv, axis=0, dtype=jnp.float32)
    back_tokens = back_pre + jnp.einsum(
        "rc,dc->rd", back_qkv, w_qkv, preferred_element_type=jnp.float32
    )
    small = lax.psum(
        (
            column_sums[:width],
            column_sums[2 * width :],
            sum_out_bias,
            back_gain_attn,
            back_shift_attn,
            sum_in_bias,
            sum_back_bias,
            back_gain_out,
            back_shift_out,
        ),
        ("dp", "head"),
    )
    matrices = (grad_w_qkv, grad_w_out, grad_w_in, grad_w_back)
    row_parts = (
        lax.psum_scatter(matrices[0], "dp", scatter_dimension=0, tiled=True),
        lax.psum_scatter(matrices[1], "dp", scatter_dimension=0, tiled=True),
        lax.psum_scatter(matrices[2], "dp", scatter_dimension=0, tiled=True),
        lax.psum_scatter(matrices[3], "dp", scatter_dimension=0, tiled=True),
    )
    shares = (
        lax.psum_scatter(
            row_parts[0].astype(jnp.bfloat16), "head", scatter_dimension=1, tiled=True
        ).astype(jnp.float32),
        lax.psum_scatter(
            row_parts[1].astype(jnp.bfloat16), "head", scatter_dimension=1, tiled=True
        ).astype(jnp.float32),
        lax.psum_scatter(
            row_parts[2].astype(jnp.bfloat16), "head", scatter_dimension=1, tiled=True
        ).astype(jnp.float32),
        lax.psum_scatter(
            row_parts[3].astype(jnp.bfloat16), "head", scatter_dimension=1, tiled=True
        ).astype(jnp.float32),
    )
    return (
        layer_out,
        back_tokens,
        shares[0],
        small[0],
        small[1],
        shares[1],
        small[2],
        small[3],
        small[4],
        shares[2],
        small[5],
        shares[3],
        small[6],
        small[7],
        small[8],
    )


def solution(mesh):
    return jax.shard_map(
        body,
        mesh=mesh,
        in_specs=(
            P(("dp", "head"), None),
            P(),
            P(),
            P(),
            P(),
            P(),
            P(),
            P(),
            P(),
            P(),
            P(),
            P(),
            P(),
            P(),
            P(("dp", "head"), None),
            P(("dp", "head")),
        ),
        out_specs=(
            P(("dp", "head"), None),
            P(("dp", "head"), None),
            P("dp", "head"),
            P(),
            P(),
            P("dp", "head"),
            P(),
            P(),
            P(),
            P("dp", "head"),
            P(),
            P("dp", "head"),
            P(),
            P(),
            P(),
        ),
        check_vma=False,
    )
```

profile of v0, /device:TPU:0, one launch (start us, length us, event | category | flops | bytes accessed | tf_op | source)
XLA Modules:
  0.0 980.4 jit_solution(3491094263376873270)
XLA Ops:
  16.6 9.9 %reshape.151 = bf16[1024,3,2,384]{3,2,1,0:T(2,128)(2,1)} reshape(bf16[1024,2304]{1,0:T(8,128)(2,1)} %add_convert_fusion.1) | data formatting | bytes 9437184 | tf_op jit(solution)/shard_map/reshape | solution.py:36
  26.5 12.5 %copy.97 = bf16[1024,3,2,384]{0,3,1,2:T(8,128)(2,1)} copy(bf16[1024,3,2,384]{3,2,1,0:T(2,128)(2,1)} %reshape.151) | data formatting | bytes 9437184 | tf_op jit(solution)/shard_map/reshape | solution.py:36
  39.0 13.2 %all_to_all.70 = bf16[1024,3,2,384]{0,3,1,2:T(8,128)(2,1)} all-to-all(bf16[1024,3,2,384]{0,3,1,2:T(8,128)(2,1)} %copy.97), channel_id=1, replica_groups=mesh['dp'=16,'head'=2] {'head'}, dimensions={2} | all-to-all | bytes 9437184 | tf_op jit(solution)/shard_map/all_to_all | solution.py:37
  52.2 9.4 copy.98
  61.6 12.0 %reshape.152 = bf16[4,512,3,6,64]{1,0,4,3,2:T(4,128)(2,1)} reshape(bf16[2,1024,3,1,384]{1,0,4,2,3:T(2,128)(2,1)} %copy.98) | data formatting | bytes 9437184 | tf_op jit(solution)/shard_map/reshape | solution.py:39
  76.9 10.1 %multiply_reduce_fusion.1 = (f32[4,6,512]{2,1,0:T(8,128)S(1)}, f32[4,6,512,512]{2,3,1,0:T(8,128)}) fusion(bf16[4,512,1,6,64]{1,0,4,3,2:T(4,128)(2,1)S(1)} %get-tuple-element.102, bf16[4,512,1,6,64]{1,0,4,3,2:T(4,128)(2,1)S(1)} %get-tuple-element.101), kind=kOutput, calls=%fused_computation.6 | convolution fusion | flops 817876992 | bytes 28360704 | tf_op jit(solution)/shard_map/sqhd,skhd->shqk/dot_general | solution.py:44
  87.0 10.5 %fusion = f32[4,6,512]{2,1,0:T(8,128)S(1)} fusion(f32[4,6,512,512]{2,3,1,0:T(8,128)} %get-tuple-element.109, f32[4,6,512]{2,1,0:T(8,128)S(1)} %get-tuple-element.108), kind=kLoop, calls=%fused_computation.5 | loop fusion | flops 18862080 | bytes 25264128 | tf_op jit(solution)/shard_map/reduce_sum | solution.py:48
  97.5 11.2 %fusion.25 = bf16[4,512,6,64]{1,3,2,0:T(8,128)(2,1)S(1)} fusion(f32[4,6,512,512]{2,3,1,0:T(8,128)} %get-tuple-element.109, f32[4,6,512]{2,1,0:T(8,128)S(1)} %fusion, f32[4,6,512]{2,1,0:T(8,128)S(1)} %get-tuple-element.108, bf16[4,512,1,6,64]{1,0,4,3,2:T(4,128)(2,1)S(1)} %get-tuple-element.100), kind=kOutput, calls=%fused_computation.67 | convolution fusion | flops 831258624 | bytes 28409856 | tf_op jit(solution)/shard_map/shqk,skhd->sqhd/dot_general | solution.py:51
  149.0 37.6 %multiply_convert_fusion.1 = (bf16[1024,3072]{1,0:T(8,128)(2,1)S(1)}, f32[1024,3072]{1,0:T(8,128)}, f32[1024,3072]{1,0:T(8,128)}) fusion(f32[3072]{0:T(1024)S(1)} %copy-done.20, bf16[768,3072]{1,0:T(8,128)(2,1)S(1)} %bitcast.100, f32[1024,768]{0,1:T(8,128)S(1)} %get-tuple-element.111, f32[768]{0:T(1024)S(1)} %copy-done.23, f32[768]{0:T(1024)S(1)} %copy-done.18, ...), kind=kOutput, calls=%fused_computation.14 | convolution fusion | flops 5043388416 | bytes 39348224 | tf_op jit(solution)/shard_map/dot_general | solution.py:62
  200.3 17.5 %convert_reduce_fusion = (f32[3072]{0:T(1024)}, bf16[1024,3072]{1,0:T(8,128)(2,1)}) fusion(f32[1024,3072]{1,0:T(8,128)} %get-tuple-element.99, bf16[1024,768]{0,1:T(8,128)(2,1)} %get-tuple-element.93, bf16[3072,768]{1,0:T(8,128)(2,1)} %param.26, f32[1024,3072]{1,0:T(8,128)} %get-tuple-element.112, f32[3072]{0:T(1024)} %param.25), kind=kOutput, calls=%fused_computation.11 | convolution fusion | flops 4885312512 | bytes 37773312 | tf_op jit(solution)/shard_map/rd,fd->rf/dot_general | solution.py:101
  217.8 12.2 %multiply_reduce_fusion.3 = (f32[768]{0:T(1024)}, f32[1024]{0:T(1024)S(1)}, f32[768]{0:T(1024)}, f32[1024,768]{0,1:T(8,128)S(1)}) fusion(f32[1024,768]{0,1:T(8,128)} %copy-done.7, f32[1024]{0:T(1024)S(1)} %fusion.30, f32[1024]{0:T(1024)S(1)} %broadcast_multiply_fusion.1, f32[768]{0:T(1024)S(1)} %copy-done.18, bf16[1024,3072]{1,0:T(8,128)(2,1)} %get-tuple-element.119, ...), kind=kOutput, calls=%fused_computation.38 | convolution fusion | flops 4845990912 | bytes 22065152 | tf_op jit(solution)/shard_map/rf,df->rd/dot_general | solution.py:106
  257.7 12.5 %fusion.20 = bf16[4,512,6,64]{1,3,2,0:T(8,128)(2,1)} fusion(f32[4,6,512,512]{2,3,1,0:T(8,128)} %get-tuple-element.109, f32[4,6,512]{2,1,0:T(8,128)} %log_add_fusion, bf16[4,512,6,64]{1,0,3,2:T(4,128)(2,1)} %reshape.156), kind=kOutput, calls=%fused_computation.64 | convolution fusion | flops 824967168 | bytes 28360704 | tf_op jit(solution)/shard_map/shqk,sqhd->skhd/dot_general | solution.py:223
  270.2 21.2 %multiply_reduce_fusion = (f32[4,6,512]{2,1,0:T(8,128)}, f32[4,6,512,512]{2,3,1,0:T(8,128)}) fusion(f32[4,6,512,512]{2,3,1,0:T(8,128)} %get-tuple-element.109, f32[4,6,512]{2,1,0:T(8,128)} %log_add_fusion, bf16[4,512,1,6,64]{1,0,4,3,2:T(4,128)(2,1)} %copy-done.9, bf16[4,512,6,64]{1,0,3,2:T(4,128)(2,1)} %reshape.156), kind=kOutput, calls=%fused_computation.1 | convolution fusion | flops 830459904 | bytes 53575680 | tf_op jit(solution)/shard_map/sqhd,skhd->shqk/dot_general | solution.py:226
  299.1 17.8 %multiply_convert_fusion = bf16[4,6,512,512]{2,3,1,0:T(8,128)(2,1)S(1)} fusion(f32[4,6,512,512]{2,3,1,0:T(8,128)} %get-tuple-element.117, f32[4,6,512,512]{2,3,1,0:T(8,128)} %get-tuple-element.109, f32[4,6,512]{2,1,0:T(8,128)} %get-tuple-element.116, f32[4,6,512]{2,1,0:T(8,128)} %log_add_fusion), kind=kLoop, calls=%fused_computation | loop fusion | flops 31457280 | bytes 63012864 | tf_op jit(solution)/shard_map/convert_element_type | solution.py:230
  327.6 9.0 fusion.24
  347.9 10.4 %copy.117 = bf16[2048,3,1,384]{3,1,2,0:T(4,128)(2,1)} copy(bf16[2048,3,1,384]{0,3,2,1:T(8,128)(2,1)} %pad_maximum_fusion) | data formatting | bytes 9437184 | tf_op jit(solution)/shard_map/stack | solution.py:239
  358.2 10.5 %all_to_all.71 = bf16[2048,3,1,384]{3,1,2,0:T(4,128)(2,1)S(1)} all-to-all(bf16[2048,3,1,384]{3,1,2,0:T(4,128)(2,1)} %copy.117), channel_id=1, replica_groups=mesh['dp'=16,'head'=2] {'head'}, dimensions={0} | all-to-all | bytes 9437184 | tf_op jit(solution)/shard_map/all_to_all | solution.py:242
  378.2 9.6 convolution_bitcast_fusion
  395.9 9.9 %fusion.46 = f32[3072,768]{1,0:T(8,128)} fusion(bf16[1024,3072]{1,0:T(8,128)(2,1)} %copy-done.24, bf16[1024,768]{0,1:T(8,128)(2,1)} %get-tuple-element.93), kind=kOutput, calls=%fused_computation.95 | convolution fusion | flops 4831838208 | bytes 17301504 | tf_op jit(solution)/shard_map/rf,rd->fd/dot_general | solution.py:100
  405.8 10.7 %fusion.34 = f32[768,3072]{1,0:T(8,128)} fusion(bf16[1024,3072]{1,0:T(8,128)(2,1)} %get-tuple-element.119, f32[1024,768]{0,1:T(8,128)} %copy-done.7, f32[768]{0:T(1024)} %param.23, f32[768]{0:T(1024)} %param.22, f32[1024]{0:T(1024)S(1)} %fusion.30, f32[1024]{0:T(1024)S(1)} %broadcast_multiply_fusion.1), kind=kOutput, calls=%fused_computation.86 | convolution fusion | flops 4835770368 | bytes 18888704 | tf_op jit(solution)/shard_map/rd,rf->df/dot_general | solution.py:105
  420.0 129.8 %reduce-scatter.25.cloned.1.call-done = f32[48,2304]{1,0:T(8,128)} async-done(((f32[768,2304]{1,0:T(8,128)}), f32[48,2304]{1,0:T(8,128)}) %reduce-scatter.25.cloned.1.call-update) | async-done | bytes 442384
  551.9 174.6 %reduce-scatter.23.cloned.1.call-done = f32[192,768]{1,0:T(8,128)} async-done(((f32[3072,768]{1,0:T(8,128)}), f32[192,768]{1,0:T(8,128)}) %reduce-scatter.23.cloned.1.call-update) | async-done | bytes 589840 | tf_op jit(solution)/shard_map/reduce_scatter | solution.py:269
  730.3 170.8 %reduce-scatter.19.cloned.1.call-done = f32[48,3072]{1,0:T(8,128)} async-done(((f32[768,3072]{1,0:T(8,128)}), f32[48,3072]{1,0:T(8,128)}) %reduce-scatter.19.cloned.1.call-update) | async-done | bytes 589840 | tf_op jit(solution)/shard_map/reduce_scatter | solution.py:268
  922.9 40.7 %all-reduce = (f32[768]{0:T(1024)}, f32[768]{0:T(1024)}, f32[768]{0:T(1024)}, f32[768]{0:T(1024)}, f32[768]{0:T(1024)}, /*index=5*/f32[3072]{0:T(1024)}, f32[768]{0:T(1024)}, f32[768]{0:T(1024)}, f32[768]{0:T(1024)}) all-reduce(f32[768]{0:T(1024)} %slice.28, f32[768]{0:T(1024)S(1)} %slice.30, ...), channel_id=1, replica_groups=mesh['dp'=16,'head'=2] {'dp','head'}, use_global_device_ids=true, to_apply=%region_14.0 | all-reduce | flops 9216 | bytes 73728 | tf_op jit(solution)/shard_map/psum | solution.py:250
  (151 shorter events, 182.2 us)
Async XLA Ops:
  76.9 10.1 %copy-start.3 = (bf16[4,512,1,6,64]{1,0,4,3,2:T(4,128)(2,1)}, bf16[4,512,1,6,64]{1,0,4,3,2:T(4,128)(2,1)S(1)}, u32[]{:S(2)}) copy-start(bf16[4,512,1,6,64]{1,0,4,3,2:T(4,128)(2,1)S(1)} %get-tuple-element.101) | copy-start | bytes 4718596
  76.9 10.1 %copy-start.4 = (bf16[4,512,1,6,64]{1,0,4,3,2:T(4,128)(2,1)}, bf16[4,512,1,6,64]{1,0,4,3,2:T(4,128)(2,1)S(1)}, u32[]{:S(2)}) copy-start(bf16[4,512,1,6,64]{1,0,4,3,2:T(4,128)(2,1)S(1)} %get-tuple-element.102) | copy-start | bytes 4718596
  76.9 20.6 %copy-start.9 = (bf16[4,512,1,6,64]{1,0,4,3,2:T(4,128)(2,1)}, bf16[4,512,1,6,64]{1,0,4,3,2:T(4,128)(2,1)S(1)}, u32[]{:S(2)}) copy-start(bf16[4,512,1,6,64]{1,0,4,3,2:T(4,128)(2,1)S(1)} %get-tuple-element.100) | copy-start | bytes 4718596
  87.0 10.5 %copy-start.12 = (f32[4,6,512]{2,1,0:T(8,128)}, f32[4,6,512]{2,1,0:T(8,128)S(1)}, u32[]{:S(2)}) copy-start(f32[4,6,512]{2,1,0:T(8,128)S(1)} %get-tuple-element.108) | copy-start | bytes 147460
  97.5 11.3 %copy-start.13 = (f32[4,6,512]{2,1,0:T(8,128)}, f32[4,6,512]{2,1,0:T(8,128)S(1)}, u32[]{:S(2)}) copy-start(f32[4,6,512]{2,1,0:T(8,128)S(1)} %fusion) | copy-start | bytes 147460
  124.5 7.4 copy-start.19
  124.5 10.0 %all-to-all-start.1 = ((bf16[2,2,196608]{2,1,0:T(2,128)(2,1)}), bf16[2,2,196608]{2,1,0:T(2,128)(2,1)}, u32[]{:S(2)}, u32[]{:S(2)}) async-start(bf16[2,2,196608]{2,1,0:T(2,128)(2,1)} %reshape.164), calls=%async_computation.1 | async-start | bytes 3145728 | tf_op jit(solution)/shard_map/all_to_all | solution.py:55
  129.3 287.4 %reduce-scatter.17.cloned.1.call-start = ((), (), s32[]{:S(2)}) async-start(), calls=%async_computation.13 | async-start | bytes 2506752 | tf_op jit(solution)/shard_map/reduce_scatter | solution.py:267
  144.1 42.5 %slice-start = ((s8[4718592]{0:T(1024)(128)(4,1)}), s8[4194304]{0:T(1024)(128)(4,1)S(1)}, s32[]{:S(2)}) async-start(s8[4718592]{0:T(1024)(128)(4,1)} %bitcast.97), calls=%async_computation.20 | async-start | bytes 8388608
  148.2 38.4 %copy-start.7 = (f32[1024,768]{0,1:T(8,128)}, f32[1024,768]{0,1:T(8,128)S(1)}, u32[]{:S(2)}) copy-start(f32[1024,768]{0,1:T(8,128)S(1)} %get-tuple-element.111) | copy-start | bytes 9437188
  149.0 37.6 %slice-start.1 = ((s8[4718592]{0:T(1024)(128)(4,1)}), s8[524288]{0:T(1024)(128)(4,1)S(1)}, s32[]{:S(2)}) async-start(s8[4718592]{0:T(1024)(128)(4,1)} %bitcast.97), calls=%async_computation.21 | async-start | bytes 1048576
  149.0 37.6 %copy-start.22 = (f32[768]{0:T(1024)S(1)}, f32[768]{0:T(1024)}, u32[]{:S(2)}) copy-start(f32[768]{0:T(1024)} %param.27) | copy-start | bytes 9220
  186.5 6.1 copy-start.24
  186.6 6.0 copy-start.2
  217.8 12.2 %copy-start.8 = (f32[1024,768]{0,1:T(8,128)S(1)}, f32[1024,768]{0,1:T(8,128)}, u32[]{:S(2)}) copy-start(f32[1024,768]{0,1:T(8,128)} %copy-done.7) | copy-start | bytes 9437188
  241.1 7.3 all-to-all-start.2
  245.8 304.0 %reduce-scatter.25.cloned.1.call-start = ((), (), s32[]{:S(2)}) async-start(), calls=%async_computation.17 | async-start | bytes 7520256
  299.1 17.8 %copy-start.5 = (bf16[4,512,1,6,64]{1,0,4,3,2:T(4,128)(2,1)S(1)}, bf16[4,512,1,6,64]{1,0,4,3,2:T(4,128)(2,1)}, u32[]{:S(2)}) copy-start(bf16[4,512,1,6,64]{1,0,4,3,2:T(4,128)(2,1)} %copy-done.4) | copy-start | bytes 4718596
  395.8 330.7 %reduce-scatter.23.cloned.1.call-start = ((), (), s32[]{:S(2)}) async-start(), calls=%async_computation.16 | async-start | bytes 10027008 | tf_op jit(solution)/shard_map/reduce_scatter | solution.py:269
  405.8 495.4 %reduce-scatter.19.cloned.1.call-start = ((), (), s32[]{:S(2)}) async-start(), calls=%async_computation.14 | async-start | bytes 10027008 | tf_op jit(solution)/shard_map/reduce_scatter | solution.py:268
  416.6 546.9 %reduce-scatter.27.cloned.1.call-start = ((), (), s32[]{:S(2)}) async-start(), calls=%async_computation.18 | async-start | bytes 294912
  420.0 546.6 %reduce-scatter.15.cloned.1.call-start = ((), (), s32[]{:S(2)}) async-start(), calls=%async_computation.12 | async-start | bytes 884736 | tf_op jit(solution)/shard_map/reduce_scatter | solution.py:272
  551.9 416.5 %reduce-scatter.29.cloned.1.call-start = ((), (), s32[]{:S(2)}) async-start(), calls=%async_computation.19 | async-start | bytes 589824
  730.3 241.4 %reduce-scatter.21.cloned.1.call-start = ((), (), s32[]{:S(2)}) async-start(), calls=%async_computation.15 | async-start | bytes 442368 | tf_op jit(solution)/shard_map/reduce_scatter | solution.py:278
  (15 other events, 49.1 us)
Sparse Core Ops, SparseCore 0:
  236.9 130.9 reduce-scatter.16
  396.0 153.7 reduce-scatter.24
  556.4 170.0 reduce-scatter.22
  732.1 169.0 reduce-scatter.18
  903.9 6.4 reduce-scatter.26
  912.6 9.1 reduce-scatter.14
  924.1 8.9 reduce-scatter.28
  935.9 8.8 reduce-scatter.20
where the time goes:
time: 986 us; the launch traced here: 980 us
  waiting for transfers between devices  476 us (48%)
  matrix products  196 us (20%)
  local copies, waits for them, and re-layouts  157 us (16%)
  blocking collectives  64.4 us (7%)
  other arithmetic  61.7 us (6%)
  between operations  14.8 us (2%)
  starting transfers between devices  9.95 us (1%)
    reduce_scatter x1, waiting for transfers between devices, body(): lax.psum_scatter(matrices[3], 'dp', scatter_dimension=0, tiled=True)  175 us
    reduce_scatter x1, waiting for transfers between devices, body(): lax.psum_scatter(matrices[2], 'dp', scatter_dimension=0, tiled=True)  171 us
    unnamed x11, waiting for transfers between devices  130 us
    unnamed x73, local copies, waits for them, and re-layouts  49 us
    psum x1, blocking collectives, body(): lax.psum((column_sums[:width], column_sums[2 * width:], sum_out_bias, bac...  40.7 us
    dot_general x1, matrix products, forward(): inner = jnp.dot(hidden_low, w_in, preferred_element_type=jnp.float32) + b_in  37.6 us
    reshape x2, local copies, waits for them, and re-layouts, forward(): projected = projected.reshape(rows, 3, halves, width // halves)  22.4 us
    another operation x4, local copies, waits for them, and re-layouts, body(): jnp.stack([back_query, back_key, back_value], axis=2)  21.8 us
  transfers between devices with their start and end apart: 10, of which 4 were waited for; matrix products, arithmetic and copies ran while one was open for 21% of the time, Pallas kernels for 0%

commit v1 on v0

v1 whole, which is shorter than its diff:
```python
import functools

import jax
import jax.numpy as jnp
from jax import lax
from jax.experimental import pallas as pl
from jax.experimental.pallas import tpu as pltpu
from jax.sharding import PartitionSpec as P

HEADS = 12
HEAD_DIM = 64
LEN = 512
CAP = 320
TILE = 64
SLOTS = (CAP // TILE + 1) * TILE
QUAD = 4 * HEAD_DIM
VMEM_LIMIT = 60 * 1024 * 1024

epsilon = 1e-12
bf16 = jnp.bfloat16
f32 = jnp.float32


def mm(a, b):
    return jnp.dot(a, b, preferred_element_type=f32)


def mm_nt(a, b):
    return lax.dot_general(a, b, (((1,), (1,)), ((), ())), preferred_element_type=f32)


def mm_tn(a, b):
    return lax.dot_general(a, b, (((0,), (0,)), ((), ())), preferred_element_type=f32)


def colsum(v):
    return jnp.sum(v, axis=0, keepdims=True)


def rowmean(v):
    return jnp.sum(v, axis=-1, keepdims=True) * (1.0 / v.shape[-1])


def norm_parts(v):
    centred = v - rowmean(v)
    r = lax.rsqrt(rowmean(centred * centred) + epsilon)
    return centred * r, r


def norm_back(cot, nhat, r, gain):
    e = cot * gain
    return r * (e - rowmean(e) - nhat * rowmean(e * nhat))


def phi_parts(v):
    x = jnp.abs(v)
    t = 1.0 / (1.0 + (0.3275911 * 0.7071067811865476) * x)
    e = jnp.exp(v * v * -0.5)
    poly = 0.5 * 1.061405429 * t + 0.5 * -1.453152027
    poly = poly * t + 0.5 * 1.421413741
    poly = poly * t + 0.5 * -0.284496736
    poly = poly * t + 0.5 * 0.254829592
    tail = poly * t * e
    return jnp.where(v >= 0.0, 1.0 - tail, tail), e


def lane_masks(dtype):
    head = lax.broadcasted_iota(jnp.int32, (1, QUAD), 1) // HEAD_DIM
    return [(head == j).astype(f32).astype(dtype) for j in range(4)]


def spread(x, masks):
    return jnp.concatenate([x * m for m in masks], axis=0)


def gather_heads(x, masks):
    n = x.shape[0] // 4
    total = x[:n] * masks[0]
    for j in range(1, 4):
        total = total + x[j * n : (j + 1) * n] * masks[j]
    return total


def softmax_rows(scores):
    e = jnp.exp(scores - jnp.max(scores, axis=-1, keepdims=True))
    return (e * (1.0 / jnp.sum(e, axis=-1, keepdims=True))).astype(bf16)


class Mover:
    def __init__(self, sems):
        self.sems = sems
        self.count = 0

    def start(self, src, dst):
        copy = pltpu.make_async_copy(src, dst, self.sems.at[self.count])
        self.count += 1
        copy.start()
        return copy


def marked_forward_kernel(
    core_ref, m_ref, bq_ref, bv_ref, bo_ref, g1_ref, s1_ref, bi_ref, bb_ref, g2_ref,
    tok_h, gout_h, wqkv_h, wout_h, win_h, wback_h,
    sel_h, kv_h, tokc_h, qs_h, p_h, ctx_h, nhat_h, r_h, hl_h, act_h, bbr_h, bin_h, bsum_h, xsend_h, small_ref,
    tok, gout, wqkv, wout, win, wback,
    sel, kv, tokc, gc, qs, prob, ctx, nhat, rr, hidden, hl, act, gp, branch, bbr, bin_, bsum, bv, bi,
    sems,
):
    rows, width = tok.shape
    ff = win.shape[1]
    mover = Mover(sems)
    other = 1 - core_ref[0]
    c_tok = mover.start(tok_h, tok)
    c_wqkv = mover.start(wqkv_h, wqkv)
    c_gout = mover.start(gout_h, gout)
    c_wout = mover.start(wout_h, wout)
    c_win = mover.start(win_h, win)
    c_wback = mover.start(wback_h, wback)
    outs = []
    bv[...] = bv_ref[...].reshape(bv.shape)
    bi[...] = bi_ref[...].reshape(bi.shape)
    m8 = m_ref[...].astype(f32)
    groups = m8.shape[0]
    per_seq = LEN // 128
    tri = (
        lax.broadcasted_iota(jnp.int32, (128, 128), 0)
        <= lax.broadcasted_iota(jnp.int32, (128, 128), 1)
    ).astype(f32).astype(bf16)
    within = mm(m8.astype(bf16), tri)
    first = jnp.sum(m8[:per_seq], axis=(0, 1), keepdims=True)
    a0 = jnp.floor((first + (TILE - 1)) * (1.0 / TILE)) * TILE
    offset = jnp.zeros((1, 1), f32)
    slot_iota = lax.broadcasted_iota(jnp.int32, (SLOTS, 128), 0).astype(f32)
    for g in range(groups):
        if g == per_seq:
            offset = a0
        slot = jnp.where(m8[g : g + 1] > 0.0, offset + within[g : g + 1] - 1.0, -1.0)
        sel[:, 128 * g : 128 * (g + 1)] = (slot_iota == slot).astype(f32).astype(bf16)
        offset = offset + within[g : g + 1, 127:128]
    outs.append(mover.start(sel, sel_h))
    a0_scalar = jnp.sum(a0).astype(jnp.int32)

    c_tok.wait()
    tokc[...] = mm(sel[...], tok[...]).astype(bf16)
    outs.append(mover.start(tokc, tokc_h))
    c_wqkv.wait()

    @pl.loop(0, 2 * width // 256)
    def _(i):
        at = pl.multiple_of(i * 256, 256)
        bias = jnp.where(i >= width // 256, bv[:, pl.ds(pl.multiple_of(lax.rem(at, width), 256), 256)], 0.0)
        kv[:, pl.ds(at, 256)] = (
            mm(tok[...], wqkv[:, pl.ds(pl.multiple_of(width + at, 256), 256)]) + bias
        ).astype(bf16)

    outs.append(mover.start(kv, kv_h))
    qs[...] = (
        (mm(tokc[...], wqkv[:, :width]) + bq_ref[...]).astype(bf16).astype(f32) * HEAD_DIM**-0.5
    ).astype(bf16)
    outs.append(mover.start(qs, qs_h))

    masks = lane_masks(bf16)
    fmasks = lane_masks(f32)

    @pl.loop(0, SLOTS // TILE)
    def _(t):
        r0 = pl.multiple_of(t * TILE, TILE)
        k0 = pl.multiple_of(jnp.where(r0 >= a0_scalar, LEN, 0), LEN)
        for g in range(width // QUAD):
            lanes = slice(g * QUAD, (g + 1) * QUAD)
            q4 = spread(qs[pl.ds(r0, TILE), lanes], masks)
            scores = mm_nt(q4, kv[pl.ds(k0, LEN), lanes])
            p = softmax_rows(scores)
            prob[t * (width // QUAD) + g] = p
            o = mm(p, kv[pl.ds(k0, LEN), width + g * QUAD : width + (g + 1) * QUAD])
            ctx[pl.ds(r0, TILE), lanes] = gather_heads(o, fmasks).astype(bf16)

    outs.append(mover.start(prob, p_h))
    outs.append(mover.start(ctx, ctx_h))
    c_wout.wait()
    pre = mm(ctx[...], wout[...]) + bo_ref[...] + tokc[...].astype(f32)
    nh, r = norm_parts(pre)
    nhat[...] = nh
    rr[...] = jnp.broadcast_to(r, rr.shape)
    outs.append(mover.start(nhat, nhat_h))
    outs.append(mover.start(rr, r_h))
    hid = nh * g1_ref[...] + s1_ref[...]
    hidden[...] = hid
    hl[...] = hid.astype(bf16)
    outs.append(mover.start(hl, hl_h))
    outs.append(mover.start(hl, xsend_h.at[:, ff : ff + width]))
    c_gout.wait()
    gc[...] = mm(sel[...], gout[...]).astype(bf16)
    c_win.wait()
    c_wback.wait()

    @pl.loop(0, ff // 256)
    def _(i):
        at = pl.ds(pl.multiple_of(i * 256, 256), 256)
        v = mm(hl[...], win[:, at]) + bi[:, at]
        cdf, e = phi_parts(v)
        act[:, at] = (v * cdf).astype(bf16)
        gp[:, at] = cdf + v * (e * 0.3989422804014327)

    outs.append(mover.start(act, act_h))
    outs.append(mover.start(act, xsend_h.at[:, :ff]))

    @pl.loop(0, width // 256)
    def _(i):
        at = pl.ds(pl.multiple_of(i * 256, 256), 256)
        branch[:, at] = mm(act[...], wback[:, at])

    nh2, r2 = norm_parts(hidden[...] + branch[...] + bb_ref[...])
    cot = gc[...].astype(f32)
    bs = norm_back(cot, nh2, r2, g2_ref[...])
    bsum[...] = bs
    outs.append(mover.start(bsum, bsum_h))
    bl = bs.astype(bf16)
    bbr[...] = bl
    outs.append(mover.start(bbr, bbr_h))
    half = width // 2
    outs.append(
        mover.start(
            bbr.at[:, pl.ds(pl.multiple_of(other * half, half), half)],
            xsend_h.at[:, ff + width : ff + width + half],
        )
    )
    small_ref[:, :width] = colsum(cot * nh2)
    small_ref[:, width : 2 * width] = colsum(cot)
    small_ref[:, 2 * width : 3 * width] = colsum(bl.astype(f32))

    @pl.loop(0, ff // 256)
    def _(i):
        start = pl.multiple_of(i * 256, 256)
        at = pl.ds(start, 256)
        b = (mm_nt(bbr[...], wback[at, :]) * gp[:, at]).astype(bf16)
        bin_[:, at] = b
        small_ref[:, pl.ds(pl.multiple_of(3 * width + start, 256), 256)] = colsum(b.astype(f32))

    outs.append(mover.start(bin_, bin_h))
    outs.append(
        mover.start(
            bin_.at[:, pl.ds(pl.multiple_of(other * (ff // 2), ff // 2), ff // 2)],
            xsend_h.at[:, ff + width + half :],
        )
    )
    for copy in outs:
        copy.wait()


def marked_forward(core, m8, tokens, gout, w_qkv, b_query, b_value, w_out, b_out, g1, s1, w_in, b_in, w_back, b_back, g2):
    rows, width = tokens.shape
    ff = w_in.shape[1]
    tiles = SLOTS // TILE * (width // QUAD)
    row = lambda v: v
    outs = dict(
        sel=((SLOTS, rows), bf16), kv=((rows, 2 * width), bf16), tokc=((SLOTS, width), bf16),
        qs=((SLOTS, width), bf16), p=((tiles, 4 * TILE, LEN), bf16), ctx=((SLOTS, width), bf16),
        nhat=((SLOTS, width), f32), r=((SLOTS, 128), f32), hl=((SLOTS, width), bf16),
        act=((SLOTS, ff), bf16), bbr=((SLOTS, width), bf16), bin=((SLOTS, ff), bf16),
        bsum=((SLOTS, width), f32), xsend=((SLOTS, (ff + width) * 3 // 2), bf16), small=((1, 3 * width + ff), f32),
    )
    scratch = [
        ((rows, width), bf16), ((rows, width), bf16), (w_qkv.shape, bf16), (w_out.shape, bf16),
        (w_in.shape, bf16), (w_back.shape, bf16),
        outs["sel"], outs["kv"], outs["tokc"], ((SLOTS, width), bf16), outs["qs"], outs["p"], outs["ctx"],
        outs["nhat"], outs["r"], ((SLOTS, width), f32), outs["hl"], outs["act"], ((SLOTS, ff), f32),
        ((SLOTS, width), f32), outs["bbr"], outs["bin"], outs["bsum"], ((1, width), f32), ((1, ff), f32),
    ]
    vmem = pl.BlockSpec(memory_space=pltpu.VMEM)
    smem = pl.BlockSpec(memory_space=pltpu.SMEM)
    hbm = pl.BlockSpec(memory_space=pl.ANY)
    res = pl.pallas_call(
        marked_forward_kernel,
        out_shape=[jax.ShapeDtypeStruct(*o) for o in outs.values()],
        in_specs=[smem] + [vmem] * 9 + [hbm] * 6,
        out_specs=[hbm] * 14 + [vmem],
        scratch_shapes=[pltpu.VMEM(*s) for s in scratch] + [pltpu.SemaphoreType.DMA((28,))],
        compiler_params=pltpu.CompilerParams(vmem_limit_bytes=VMEM_LIMIT),
        cost_estimate=pl.CostEstimate(flops=12 * 10**9, bytes_accessed=40 * 10**6, transcendentals=0),
        name="marked_forward",
    )(core, m8, row(b_query), row(b_value), row(b_out), row(g1), row(s1), row(b_in), row(b_back), row(g2),
      tokens, gout, w_qkv, w_out, w_in, w_back)
    return dict(zip(outs, res))


def marked_backward_kernel(
    m_ref, g1_ref,
    win_h, wout_h, wqkv_h, bin_h, bsum_h, nhat_h, r_h, ctx_h, p_h, qs_h, kv_h,
    battn_h, bq_h, bkv_h, rc_h, small_ref,
    win, wout, wq, bin_, bsum, nhat, rr, ctx, prob, qs, kv,
    bh, bpre, battn, bctx, dk, dv, bq, bkv, rc,
    sems,
):
    rows, width = kv.shape[0], qs.shape[1]
    mover = Mover(sems)
    c_bin = mover.start(bin_h, bin_)
    c_win = mover.start(win_h, win)
    c_bsum = mover.start(bsum_h, bsum)
    c_nhat = mover.start(nhat_h, nhat)
    c_r = mover.start(r_h, rr)
    c_wout = mover.start(wout_h, wout)
    c_att = [mover.start(s, d) for s, d in ((ctx_h, ctx), (p_h, prob), (qs_h, qs), (kv_h, kv))]
    c_wq = mover.start(wqkv_h.at[:, :width], wq)
    outs = []
    per_seq = LEN // 128
    first = jnp.sum(m_ref[:per_seq].astype(f32), axis=(0, 1), keepdims=True)
    a0_scalar = jnp.sum(jnp.floor((first + (TILE - 1)) * (1.0 / TILE)) * TILE).astype(jnp.int32)
    dk[...] = jnp.zeros_like(dk)
    dv[...] = jnp.zeros_like(dv)
    for c in (c_bin, c_win, c_bsum):
        c.wait()

    @pl.loop(0, width // 256)
    def _(i):
        at = pl.ds(pl.multiple_of(i * 256, 256), 256)
        bh[:, at] = bsum[:, at] + mm_nt(bin_[...], win[at, :])

    c_nhat.wait()
    c_r.wait()
    back_hidden = bh[...]
    nh = nhat[...]
    bp = norm_back(back_hidden, nh, rr[:, :1], g1_ref[...])
    bpre[...] = bp
    bl = bp.astype(bf16)
    battn[...] = bl
    outs.append(mover.start(battn, battn_h))
    small_ref[:, :width] = colsum(bl.astype(f32))
    small_ref[:, width : 2 * width] = colsum(back_hidden * nh)
    small_ref[:, 2 * width : 3 * width] = colsum(back_hidden)
    c_wout.wait()
    bctx[...] = mm_nt(bl, wout[...]).astype(bf16)
    for c in c_att:
        c.wait()
    masks = lane_masks(bf16)
    fmasks = lane_masks(f32)

    @pl.loop(0, SLOTS // TILE)
    def _(t):
        r0 = pl.multiple_of(t * TILE, TILE)
        k0 = pl.multiple_of(jnp.where(r0 >= a0_scalar, LEN, 0), LEN)
        for g in range(width // QUAD):
            lanes = slice(g * QUAD, (g + 1) * QUAD)
            d = bctx[pl.ds(r0, TILE), lanes]
            d4 = spread(d, masks)
            q4 = spread(qs[pl.ds(r0, TILE), lanes], masks)
            prod = d.astype(f32) * ctx[pl.ds(r0, TILE), lanes].astype(f32)
            delta = jnp.concatenate(
                [jnp.sum(prod * m, axis=-1, keepdims=True) for m in fmasks], axis=0
            )
            p = prob[t * (width // QUAD) + g]
            dp = mm_nt(d4, kv[pl.ds(k0, LEN), width + g * QUAD : width + (g + 1) * QUAD])
            ds = (p.astype(f32) * (dp - delta)).astype(bf16)
            dv[pl.ds(k0, LEN), lanes] += mm_tn(p, d4)
            dk[pl.ds(k0, LEN), lanes] += mm_tn(ds, q4)
            o = mm(ds, kv[pl.ds(k0, LEN), lanes])
            bq[pl.ds(r0, TILE), lanes] = (gather_heads(o, fmasks) * HEAD_DIM**-0.5).astype(bf16)

    outs.append(mover.start(bq, bq_h))
    c_wq.wait()
    rc[...] = (bpre[...] + mm_nt(bq[...], wq[...])).astype(bf16)
    outs.append(mover.start(rc, rc_h))
    bkv[:, :width] = dk[...].astype(bf16)
    bvl = dv[...].astype(bf16)
    bkv[:, width:] = bvl
    outs.append(mover.start(bkv, bkv_h))
    small_ref[:, 3 * width : 4 * width] = colsum(bq[...].astype(f32))
    small_ref[:, 4 * width :] = colsum(bvl.astype(f32))
    for copy in outs:
        copy.wait()


def marked_backward(m8, g1, w_in, w_out, w_qkv, a):
    rows = a["sel"].shape[1]
    width, ff = w_in.shape
    outs = dict(
        battn=((SLOTS, width), bf16), bq=((SLOTS, width), bf16), bkv=((rows, 2 * width), bf16),
        rc=((SLOTS, width), bf16), small=((1, 5 * width), f32),
    )
    ins = [a[k] for k in ("bin", "bsum", "nhat", "r", "ctx", "p", "qs", "kv")]
    scratch = [(w_in.shape, bf16), (w_out.shape, bf16), ((width, width), bf16)]
    scratch += [(v.shape, v.dtype) for v in ins]
    scratch += [
        ((SLOTS, width), f32), ((SLOTS, width), f32), outs["battn"], ((SLOTS, width), bf16),
        ((rows, width), f32), ((rows, width), f32), outs["bq"], outs["bkv"], outs["rc"],
    ]
    vmem = pl.BlockSpec(memory_space=pltpu.VMEM)
    smem = pl.BlockSpec(memory_space=pltpu.SMEM)
    hbm = pl.BlockSpec(memory_space=pl.ANY)
    res = pl.pallas_call(
        marked_backward_kernel,
        out_shape=[jax.ShapeDtypeStruct(*o) for o in outs.values()],
        in_specs=[vmem] * 2 + [hbm] * 11,
        out_specs=[hbm] * 4 + [vmem],
        scratch_shapes=[pltpu.VMEM(*s) for s in scratch] + [pltpu.SemaphoreType.DMA((28,))],
        compiler_params=pltpu.CompilerParams(vmem_limit_bytes=VMEM_LIMIT),
        cost_estimate=pl.CostEstimate(flops=8 * 10**9, bytes_accessed=40 * 10**6, transcendentals=0),
        name="marked_backward",
    )(m8, g1, w_in, w_out, w_qkv, *ins)
    return dict(zip(outs, res))


BLOCK = 256


def layer_rows_kernel(
    which, bq_ref, bo_ref, g1_ref, s1_ref, bi_ref, bb_ref, g2_ref, s2_ref,
    tok_h, kv_h, wqkv_h, wout_h, win_h, wback_h, *rest,
):
    (out_h, tok, kv, wq, wout, win, wback, q, ctx, hl, hidden, act, branch, out, bi, sems) = rest[-16:]
    width = wq.shape[1]
    ff = win.shape[1]
    mover = Mover(sems)
    i = which[0]
    r0 = pl.multiple_of(i * BLOCK, BLOCK)
    k0 = pl.multiple_of(i // (LEN // BLOCK) * LEN, LEN)
    c_tok = mover.start(tok_h.at[pl.ds(r0, BLOCK), :], tok)
    c_wq = mover.start(wqkv_h.at[:, :width], wq)
    c_kv = mover.start(kv_h.at[pl.ds(k0, LEN), :], kv)
    c_wout = mover.start(wout_h, wout)
    c_win = mover.start(win_h, win)
    c_wback = mover.start(wback_h, wback)
    bi[...] = bi_ref[...].reshape(bi.shape)
    c_tok.wait()
    c_wq.wait()
    q[...] = ((mm(tok[...], wq[...]) + bq_ref[...]).astype(bf16).astype(f32) * HEAD_DIM**-0.5).astype(bf16)
    c_kv.wait()
    masks = lane_masks(bf16)
    fmasks = lane_masks(f32)

    @pl.loop(0, BLOCK // TILE)
    def _(t):
        at = pl.ds(pl.multiple_of(t * TILE, TILE), TILE)
        for g in range(width // QUAD):
            lanes = slice(g * QUAD, (g + 1) * QUAD)
            p = softmax_rows(mm_nt(spread(q[at, lanes], masks), kv[:, lanes]))
            o = mm(p, kv[:, width + g * QUAD : width + (g + 1) * QUAD])
            ctx[at, lanes] = gather_heads(o, fmasks).astype(bf16)

    c_wout.wait()
    nh, _ = norm_parts(mm(ctx[...], wout[...]) + bo_ref[...] + tok[...].astype(f32))
    hid = nh * g1_ref[...] + s1_ref[...]
    hidden[...] = hid
    hl[...] = hid.astype(bf16)
    c_win.wait()

    @pl.loop(0, ff // 256)
    def _(j):
        at = pl.ds(pl.multiple_of(j * 256, 256), 256)
        v = mm(hl[...], win[:, at]) + bi[:, at]
        act[:, at] = (v * phi_parts(v)[0]).astype(bf16)

    c_wback.wait()

    @pl.loop(0, width // 256)
    def _(j):
        at = pl.ds(pl.multiple_of(j * 256, 256), 256)
        branch[:, at] = mm(act[...], wback[:, at])

    nh2, _ = norm_parts(hidden[...] + branch[...] + bb_ref[...])
    out[...] = (nh2 * g2_ref[...] + s2_ref[...]).astype(bf16)
    mover.start(out, out_h.at[pl.ds(r0, BLOCK), :]).wait()


def layer_rows(which, previous, tokens, kv, w_qkv, b_query, w_out, b_out, g1, s1, w_in, b_in, w_back, b_back, g2, s2):
    rows, width = tokens.shape
    ff = w_in.shape[1]
    row = lambda v: v
    vmem = pl.BlockSpec(memory_space=pltpu.VMEM)
    smem = pl.BlockSpec(memory_space=pltpu.SMEM)
    hbm = pl.BlockSpec(memory_space=pl.ANY)
    scratch = [
        ((BLOCK, width), bf16), ((LEN, 2 * width), bf16), ((width, width), bf16), (w_out.shape, bf16),
        (w_in.shape, bf16), (w_back.shape, bf16), ((BLOCK, width), bf16), ((BLOCK, width), bf16),
        ((BLOCK, width), bf16), ((BLOCK, width), f32), ((BLOCK, ff), bf16), ((BLOCK, width), f32),
        ((BLOCK, width), bf16), ((1, ff), f32),
    ]
    extra = () if previous is None else (previous,)
    return pl.pallas_call(
        layer_rows_kernel,
        out_shape=jax.ShapeDtypeStruct((rows, width), bf16),
        in_specs=[smem] + [vmem] * 8 + [hbm] * (6 + len(extra)),
        out_specs=hbm,
        scratch_shapes=[pltpu.VMEM(*s) for s in scratch] + [pltpu.SemaphoreType.DMA((8,))],
        input_output_aliases={15: 0} if extra else {},
        compiler_params=pltpu.CompilerParams(vmem_limit_bytes=VMEM_LIMIT),
        cost_estimate=pl.CostEstimate(flops=3 * 10**9, bytes_accessed=20 * 10**6, transcendentals=0),
        name="layer_rows",
    )(jnp.full((1,), which, jnp.int32), row(b_query), row(b_out), row(g1), row(s1), row(b_in), row(b_back), row(g2), row(s2),
      tokens, kv, w_qkv, w_out, w_in, w_back, *extra)


def place(piece, own, order):
    bits = piece ^ own
    spot = 0
    for step in order:
        spot = spot * 2 + ((bits >> step) & 1)
    return spot


def store_pieces(ref, value, first, size, own, order, lanes):
    for k in range(value.shape[0] // size):
        at = pl.multiple_of(place(first + k, own, order) * size, size)
        ref[pl.ds(at, size), lanes] = value[k * size : (k + 1) * size]


def ffn_grads_kernel(
    where, act_h, hl_h, bbr_h, bin_h, x_h, keep1_h, send1_h, keep2_h, send2_h,
    act, hl, bbr, bin_, out1, out2, sems, *, pieces, orders,
):
    own, core = where[0], where[1]
    slots, ff = act_h.shape
    width = hl_h.shape[1]
    half = width // 2
    mover = Mover(sems)
    up, down = slice(0, slots), slice(slots, 2 * slots)
    mine = lambda n: pl.ds(pl.multiple_of(core * n, n), n)
    c1 = [
        mover.start(act_h, act.at[up, :]),
        mover.start(x_h.at[:, :ff], act.at[down, :]),
        mover.start(bbr_h.at[:, mine(half)], bbr.at[up, :]),
        mover.start(x_h.at[:, ff + width : ff + width + half], bbr.at[down, :]),
    ]
    c2 = [
        mover.start(hl_h, hl.at[up, :]),
        mover.start(x_h.at[:, ff : ff + width], hl.at[down, :]),
        mover.start(bin_h.at[:, mine(ff // 2)], bin_.at[up, :]),
        mover.start(x_h.at[:, ff + width + half :], bin_.at[down, :]),
    ]
    for c in c1:
        c.wait()
    size = ff // pieces
    step = 384

    @pl.loop(0, ff // step)
    def _(j):
        g = mm_tn(act[:, pl.ds(pl.multiple_of(j * step, step), step)], bbr[...]).astype(bf16)
        store_pieces(out1, g, j * (step // size), size, own, orders[0], slice(None))

    rows = ff // 2
    outs = [mover.start(out1.at[rows:, :], send1_h), mover.start(out1.at[:rows, :], keep1_h)]
    for c in c2:
        c.wait()
    size = width // pieces
    for i in range(width // step):
        hlt = hl[:, i * step : (i + 1) * step].T

        @pl.loop(0, ff // 2 // 512)
        def _(j):
            lanes = pl.ds(pl.multiple_of(j * 512, 512), 512)
            g = mm(hlt, bin_[:, lanes]).astype(bf16)
            store_pieces(out2, g, i * (step // size), size, own, orders[1], lanes)

    outs += [mover.start(out2.at[half:, :], send2_h), mover.start(out2.at[:half, :], keep2_h)]
    for c in outs:
        c.wait()


def ffn_grads(where, a, x, pieces, orders):
    slots, ff = a["act"].shape
    width = a["hl"].shape[1]
    smem = pl.BlockSpec(memory_space=pltpu.SMEM)
    hbm = pl.BlockSpec(memory_space=pl.ANY)
    one, two = (ff // 2, width // 2), (width // 2, ff // 2)
    scratch = [
        (2 * slots, ff), (2 * slots, width), (2 * slots, width // 2), (2 * slots, ff // 2),
        (ff, width // 2), (width, ff // 2),
    ]
    return pl.pallas_call(
        functools.partial(ffn_grads_kernel, pieces=pieces, orders=orders),
        out_shape=[jax.ShapeDtypeStruct(s, bf16) for s in (one, one, two, two)],
        in_specs=[smem] + [hbm] * 5,
        out_specs=[hbm] * 4,
        scratch_shapes=[pltpu.VMEM(s, bf16) for s in scratch] + [pltpu.SemaphoreType.DMA((12,))],
        compiler_params=pltpu.CompilerParams(vmem_limit_bytes=VMEM_LIMIT),
        cost_estimate=pl.CostEstimate(flops=4 * 10**9, bytes_accessed=15 * 10**6, transcendentals=0),
        name="ffn_grads",
    )(where, a["act"], a["hl"], a["bbr"], a["bin"], x)


def projection_grads_kernel(
    where, tokc_h, bq_h, ctx_h, battn_h, tok_h, bkv_h, keep_h, send_h,
    tokc, bq, ctx, battn, tok, bkv, tokt, out, sems, *, pieces, order,
):
    own, core = where[0], where[1]
    width = tok.shape[1]
    half = width // 2
    size = width // pieces
    mover = Mover(sems)
    c1 = [mover.start(tok_h, tok), mover.start(bkv_h, bkv)]
    c2 = [mover.start(tokc_h, tokc), mover.start(bq_h, bq)]
    c3 = [mover.start(ctx_h, ctx), mover.start(battn_h, battn)]

    def products(left, right, columns, first, lanes):
        for i in range(2):
            g = mm(left[i * half : (i + 1) * half, :], right[:, columns]).astype(bf16)
            for k in range(half // size):
                at = pl.multiple_of(place(i * (half // size) + k, own, order) * size, size)
                out[first, pl.ds(at, size), lanes] = g[k * size : (k + 1) * size]

    for c in c1:
        c.wait()
    tokt[...] = tok[...].T

    @pl.loop(2, 6)
    def _(j):
        columns = pl.ds(pl.multiple_of((j - 2) * half, half), half)
        lanes = pl.ds(pl.multiple_of(lax.rem(j, 3) * half, half), half)
        products(tokt, bkv, columns, (j // 3) ^ core, lanes)

    for c in c2:
        c.wait()
    tokt[:, : tokc.shape[0]] = tokc[...].T
    short = tokt.at[:, : tokc.shape[0]]
    for j in range(2):
        columns = slice(j * half, (j + 1) * half)
        products(short, bq, columns, core, columns)
    for c in c3:
        c.wait()
    tokt[:, : tokc.shape[0]] = ctx[...].T
    for j in range(2):
        products(short, battn, slice(j * half, (j + 1) * half), j ^ core, slice(3 * half, 4 * half))
    outs = [mover.start(out.at[1], send_h), mover.start(out.at[0], keep_h)]
    for c in outs:
        c.wait()


def projection_grads(where, tokens, a, b, pieces, order):
    rows, width = tokens.shape
    smem = pl.BlockSpec(memory_space=pltpu.SMEM)
    hbm = pl.BlockSpec(memory_space=pl.ANY)
    shape = (width, 2 * width)
    ins = [a["tokc"], b["bq"], a["ctx"], b["battn"], tokens, b["bkv"]]
    scratch = [v.shape for v in ins] + [(width, rows), (2,) + shape]
    return pl.pallas_call(
        functools.partial(projection_grads_kernel, pieces=pieces, order=order),
        out_shape=[jax.ShapeDtypeStruct(shape, bf16)] * 2,
        in_specs=[smem] + [hbm] * 6,
        out_specs=[hbm] * 2,
        scratch_shapes=[pltpu.VMEM(s, bf16) for s in scratch] + [pltpu.SemaphoreType.DMA((8,))],
        compiler_params=pltpu.CompilerParams(vmem_limit_bytes=VMEM_LIMIT),
        cost_estimate=pl.CostEstimate(flops=4 * 10**9, bytes_accessed=15 * 10**6, transcendentals=0),
        name="projection_grads",
    )(where, *ins)


def add_low(a, b):
    return (a.astype(f32) + b.astype(f32)).astype(bf16)


def swap(value, bit, n):
    return lax.ppermute(value, "dp", [(i, i ^ (1 << bit)) for i in range(n)])


def reduce_pieces(keep, send, order, n):
    for i, bit in enumerate(order):
        got = swap(send, bit, n)
        if i == len(order) - 1:
            return keep.astype(f32) + got.astype(f32)
        m = keep.shape[0] // 2
        send, keep = add_low(keep[m:], got[m:]), add_low(keep[:m], got[:m])


def body(
    tokens, w_qkv, b_query, b_value, w_out, b_out, gain_attn, shift_attn, w_in, b_in, w_back, b_back,
    gain_out, shift_out, grad_out, masked,
):
    rows, width = tokens.shape
    ff = w_in.shape[1]
    n = lax.axis_size("dp")
    core = lax.axis_index("head")
    steps = n.bit_length() - 1
    halving = n == 1 << steps and width // n % 16 == 0
    if halving:
        own = lax.axis_index("dp")
        orders = [tuple(range(steps)), (1, 0) + tuple(range(2, steps)), (2, 0, 1) + tuple(range(3, steps))]
        pieces = n
    else:
        own = jnp.int32(0)
        orders = [(2, 1, 0)] * 3
        pieces = 8
    where = jnp.stack([own, core]).astype(jnp.int32)
    m8 = masked.reshape(-1, 128)
    a = marked_forward(
        core.reshape(1).astype(jnp.int32), m8, tokens, grad_out, w_qkv, b_query, b_value, w_out, b_out,
        gain_attn, shift_attn, w_in, b_in, w_back, b_back, gain_out,
    )
    x = lax.ppermute(a["xsend"], "head", [(0, 1), (1, 0)])
    b = marked_backward(m8, gain_attn, w_in, w_out, w_qkv, a)
    keep1, send1, keep2, send2 = ffn_grads(where, a, x, pieces, orders)
    keep3, send3 = projection_grads(where, tokens, a, b, pieces, orders[2])
    got3 = lax.ppermute(send3, "head", [(0, 1), (1, 0)])
    m = width // 2
    if halving:
        grad_w_back = reduce_pieces(keep1, send1, orders[0], n)
        grad_w_in = reduce_pieces(keep2, send2, orders[1], n)
        send3, keep3 = add_low(keep3[m:], got3[m:]), add_low(keep3[:m], got3[:m])
        shares = reduce_pieces(keep3, send3, orders[2], n)
    else:
        total = lambda *parts: lax.psum_scatter(
            jnp.concatenate(parts), "dp", scatter_dimension=0, tiled=True
        ).astype(f32)
        grad_w_back = total(keep1, send1)
        grad_w_in = total(keep2, send2)
        shares = total(add_low(keep3, got3))
    small = jnp.concatenate([a["small"][0], b["small"][0]])
    small = jnp.sum(lax.all_gather(small.reshape(-1, 128), ("dp", "head")), axis=0).reshape(-1)
    small_a, small_b = small[: 3 * width + ff], small[3 * width + ff :]
    layer_out = None
    for i in range(rows // BLOCK):
        layer_out = layer_rows(
            i, layer_out, tokens, a["kv"], w_qkv, b_query, w_out, b_out, gain_attn, shift_attn, w_in, b_in,
            w_back, b_back, gain_out, shift_out,
        )
    grad_tokens = mm_tn(a["sel"], b["rc"]) + mm_nt(b["bkv"], w_qkv[:, width:])
    return (
        layer_out,
        grad_tokens,
        shares[:, : 3 * m],
        small_b[3 * width : 4 * width],
        small_b[4 * width :],
        shares[:, 3 * m :],
        small_b[:width],
        small_b[width : 2 * width],
        small_b[2 * width : 3 * width],
        grad_w_in,
        small_a[3 * width :],
        grad_w_back,
        small_a[2 * width : 3 * width],
        small_a[:width],
        small_a[width : 2 * width],
    )


def solution(mesh):
    rows = P(("dp", "head"), None)
    shard = P("dp", "head")
    return jax.shard_map(
        body,
        mesh=mesh,
        in_specs=(rows,) + (P(),) * 13 + (rows, P(("dp", "head"))),
        out_specs=(rows, rows, shard, P(), P(), shard, P(), P(), P(), shard, P(), shard, P(), P(), P()),
        check_vma=False,
    )
```

time: 986 us -> 257 us (0.26)
  waiting for transfers between devices: 476 us -> 58.1 us
  matrix products: 196 us -> 7.41 us
  local copies, waits for them, and re-layouts: 157 us -> 2.61 us
  Pallas kernels: 0 us -> 143 us
  blocking collectives: 64.4 us -> 0 us
  other arithmetic: 61.7 us -> 10.6 us
  starting transfers between devices: 9.95 us -> 20.5 us
    reduce_scatter x5 -> x0, waiting for transfers between devices: 345 us -> none  [the longest x1 175 us: body(): lax.psum_scatter(matrices[3], 'dp', scatter_dimension=0, tiled=True)]
    dot_general x18 -> x2, matrix products: 196 us -> 7.41 us  [the longest x1 4.67 us: mm_nt(): lax.dot_general(a, b, (((1,), (1,)), ((), ())), preferred_element_type=f32)]
    pallas_call x0 -> x8, Pallas kernels: none -> 143 us  [the longest x4 64.7 us: layer_rows(): pl.pallas_call(layer_rows_kernel, out_shape=jax.ShapeDtypeStruct((rows, w...]
    unnamed x11 -> x1, waiting for transfers between devices: 130 us -> 0.02 us
    ppermute x0 -> x14, waiting for transfers between devices: none -> 58.1 us  [the longest x12 58.1 us: swap(): return lax.ppermute(value, 'dp', [(i, i ^ 1 << bit) for i in range(n)])]
    unnamed x73 -> x18, local copies, waits for them, and re-layouts: 49 us -> 0.04 us
    reshape x6 -> x0, local copies, waits for them, and re-layouts: 43.8 us -> none  [the longest x2 22.4 us: forward(): projected = projected.reshape(rows, 3, halves, width // halves)]
    psum x1 -> x0, blocking collectives: 40.7 us -> none  [body(): lax.psum((column_sums[:width], column_sums[2 * width:], sum_out_bias, bac...]
  transfers between devices with their start and end apart: 10 -> 15, of which waited for: 4 -> 9; matrix products, arithmetic and copies ran while one was open for 21% -> 7% of each run, Pallas kernels for 0% -> 30%
where the time goes in v1:
time: 257 us; the launch traced here: 256 us
  Pallas kernels  143 us (56%)
  waiting for transfers between devices  58.1 us (23%)
  starting transfers between devices  20.5 us (8%)
  between operations  14.3 us (6%)
  other arithmetic  10.6 us (4%)
  matrix products  7.41 us (3%)
  local copies, waits for them, and re-layouts  2.61 us (1%)
    pallas_call x4, Pallas kernels, layer_rows(): pl.pallas_call(layer_rows_kernel, out_shape=jax.ShapeDtypeStruct((rows, w...  64.7 us
    ppermute x12, waiting for transfers between devices, swap(): return lax.ppermute(value, 'dp', [(i, i ^ 1 << bit) for i in range(n)])  58.1 us
    pallas_call x1, Pallas kernels, marked_forward(): pl.pallas_call(marked_forward_kernel, out_shape=[jax.ShapeDtypeStruct(*o)...  34.6 us
    ppermute x12, starting transfers between devices, swap(): return lax.ppermute(value, 'dp', [(i, i ^ 1 << bit) for i in range(n)])  19.8 us
    pallas_call x1, Pallas kernels, marked_backward(): pl.pallas_call(marked_backward_kernel, out_shape=[jax.ShapeDtypeStruct(*o...  19.4 us
    pallas_call x1, Pallas kernels, ffn_grads(): pl.pallas_call(functools.partial(ffn_grads_kernel, pieces=pieces, orders=...  12.1 us
    pallas_call x1, Pallas kernels, projection_grads(): pl.pallas_call(functools.partial(projection_grads_kernel, pieces=pieces,...  11.9 us
    convert_element_type x10, other arithmetic, add_low(): return (a.astype(f32) + b.astype(f32)).astype(bf16)  6.34 us
  transfers between devices with their start and end apart: 15, of which 9 were waited for; matrix products, arithmetic and copies ran while one was open for 7% of the time, Pallas kernels for 30%

profile of v1, /device:TPU:0, one launch (start us, length us, event | category | flops | bytes accessed | tf_op | source)
XLA Modules:
  0.0 256.2 jit_solution(7087307121098295457)
XLA Ops:
  7.8 34.6 %marked_forward.1 = (bf16[384,1024]{1,0:T(8,128)(2,1)}, bf16[1024,1536]{1,0:T(8,128)(2,1)}, bf16[384,768]{1,0:T(8,128)(2,1)}, bf16[384,768]{1,0:T(8,128)(2,1)}, ...) custom-call(s32[1]{0:T(128)} %bitcast.core_ref, ...), custom_call_target="tpu_custom_call" | custom-call | flops 12000000000 | bytes 40000000 | tf_op jit(solution)/shard_map/marked_forward/pallas_call | solution.py:273
  42.4 19.4 %marked_backward.1 = (bf16[384,768]{1,0:T(8,128)(2,1)}, bf16[384,768]{1,0:T(8,128)(2,1)}, bf16[1024,1536]{1,0:T(8,128)(2,1)}, bf16[384,768]{1,0:T(8,128)(2,1)}, f32[1,3840]{1,0:T(1,128)}) custom-call(s32[8,128]{1,0:T(8,128)} %bitcast.27, f32[768]{0:T(1024)} %g1_ref.11, bf16[768,3072]{1,0:T(8,128)(2,1)} %win_h.11, bf16[768,768]{1,0:T(8,128)(2,1)} %wout_h.11, ...), custom_call_target="tpu_custom_call" | custom-call | flops 8000000000 | bytes 40000000 | tf_op jit(solution)/shard_map/marked_backward/pallas_call | solution.py:390
  61.9 11.9 %projection_grads.1 = (bf16[768,1536]{1,0:T(8,128)(2,1)}, bf16[768,1536]{1,0:T(8,128)(2,1)}) custom-call(s32[2]{0:T(128)} %pad_add_fusion.where, bf16[384,768]{1,0:T(8,128)(2,1)} %get-tuple-element.52.tokc_h, bf16[384,768]{1,0:T(8,128)(2,1)} %get-tuple-element.53.bq_h, bf16[384,768]{1,0:T(8,128)(2,1)} %get-tuple-element.47.ctx_h, ...), custom_call_target="tpu_custom_call" | custom-call | flops 4000000000 | bytes 15000000 | tf_op jit(solution)/shard_map/projection_grads/pallas_call | solution.py:635
  75.2 16.1 %layer_rows.4.rest_0_ = bf16[1024,768]{1,0:T(8,128)(2,1)} custom-call(s32[1]{0:T(128)} %constant.6.clone.1.which, f32[768]{0:T(1024)} %bq_ref.9, f32[768]{0:T(1024)} %bo_ref.9, f32[768]{0:T(1024)} %g1_ref.11, f32[768]{0:T(1024)} %s1_ref.9, f32[3072]{0:T(1024)} %bi_ref.9, f32[768]{0:T(1024)} %bb_ref.9, f32[768]{0:T(1024)} %g2_ref.9, f32[768]{0:T(1024)} %s2_ref.7, ...), custom_call_target="tpu_custom_call" | custom-call | flops 3000000000 | bytes 20000000 | tf_op jit(solution)/shard_map/layer_rows/pallas_call | solution.py:479
  91.3 16.2 %layer_rows.5.rest_0_ = bf16[1024,768]{1,0:T(8,128)(2,1)} custom-call(s32[1]{0:T(128)} %constant.5.clone.1.which, f32[768]{0:T(1024)} %bq_ref.9, f32[768]{0:T(1024)} %bo_ref.9, f32[768]{0:T(1024)} %g1_ref.11, f32[768]{0:T(1024)} %s1_ref.9, f32[3072]{0:T(1024)} %bi_ref.9, f32[768]{0:T(1024)} %bb_ref.9, f32[768]{0:T(1024)} %g2_ref.9, ...), custom_call_target="tpu_custom_call", output_to_operand_aliasing={{}: (15, {})} | custom-call | flops 3000000000 | bytes 20000000 | tf_op jit(solution)/shard_map/layer_rows/pallas_call | solution.py:479
  107.5 3.6 %add_convert_fusion.1 = (bf16[384,1536]{1,0:T(8,128)(2,1)}, bf16[384,1536]{1,0:T(8,128)(2,1)}) fusion(bf16[768,1536]{1,0:T(8,128)(2,1)} %collective-permute-done, bf16[768,1536]{1,0:T(8,128)(2,1)S(1)} %copy-done.2), kind=kLoop, calls=%fused_computation.1 | loop fusion | flops 4718592 | bytes 7077888 | tf_op jit(solution)/shard_map/convert_element_type | solution.py:648
  111.2 3.0 %collective-permute-start.1 = (bf16[384,1536]{1,0:T(8,128)(2,1)}, bf16[384,1536]{1,0:T(8,128)(2,1)}, u32[]{:S(2)}, u32[]{:S(2)}) collective-permute-start(bf16[384,1536]{1,0:T(8,128)(2,1)} %get-tuple-element.68), channel_id=1, source_target_pairs={{0,8},{2,10},{4,12},{6,14},{8,0},{10,2},{12,4},{14,6},{16,24},{18,... | collective-permute-start | bytes 3538952 | tf_op jit(solution)/shard_map/ppermute | solution.py:652
  114.2 16.3 %layer_rows.6.rest_0_ = bf16[1024,768]{1,0:T(8,128)(2,1)} custom-call(s32[1]{0:T(128)} %constant.4.clone.1.which, f32[768]{0:T(1024)} %bq_ref.9, f32[768]{0:T(1024)} %bo_ref.9, f32[768]{0:T(1024)} %g1_ref.11, f32[768]{0:T(1024)} %s1_ref.9, f32[3072]{0:T(1024)} %bi_ref.9, f32[768]{0:T(1024)} %bb_ref.9, f32[768]{0:T(1024)} %g2_ref.9, ...), custom_call_target="tpu_custom_call", output_to_operand_aliasing={{}: (15, {})} | custom-call | flops 3000000000 | bytes 20000000 | tf_op jit(solution)/shard_map/layer_rows/pallas_call | solution.py:479
  130.5 4.7 %fusion = f32[1024,768]{1,0:T(8,128)S(1)} fusion(bf16[1024,1536]{1,0:T(8,128)(2,1)} %get-tuple-element.51.bkv_h, bf16[768,2304]{1,0:T(8,128)(2,1)S(1)} %copy-done), kind=kOutput, calls=%fused_computation.2 | convolution fusion | flops 2415919104 | bytes 8650752 | tf_op jit(solution)/shard_map/dot_general | solution.py:29
  135.2 2.7 %convolution_add_fusion = f32[1024,768]{1,0:T(8,128)} fusion(f32[1024,768]{1,0:T(8,128)S(1)} %fusion, bf16[384,1024]{1,0:T(8,128)(2,1)S(1)} %copy-done.5, bf16[384,768]{1,0:T(8,128)(2,1)S(1)} %copy-done.6), kind=kOutput, calls=%fused_computation.4 | convolution fusion | flops 604766208 | bytes 7667712 | tf_op jit(solution)/shard_map/dot_general | solution.py:33
  138.0 5.9 %collective-permute-done.1 = bf16[384,1536]{1,0:T(8,128)(2,1)} collective-permute-done((bf16[384,1536]{1,0:T(8,128)(2,1)}, bf16[384,1536]{1,0:T(8,128)(2,1)}, u32[]{:S(2)}, u32[]{:S(2)}) %collective-permute-start.1) | collective-permute-done | bytes 1179680 | tf_op jit(solution)/shard_map/ppermute | solution.py:652
  145.4 1.7 collective-permute-start.2
  147.1 12.1 %ffn_grads.1 = (bf16[1536,384]{1,0:T(8,128)(2,1)}, bf16[1536,384]{1,0:T(8,128)(2,1)}, bf16[384,1536]{1,0:T(8,128)(2,1)}, bf16[384,1536]{1,0:T(8,128)(2,1)}) custom-call(s32[2]{0:T(128)} %pad_add_fusion.where, bf16[384,3072]{1,0:T(8,128)(2,1)} %get-tuple-element.59.act_h, bf16[384,768]{1,0:T(8,128)(2,1)} %get-tuple-element.60.hl_h, ...), custom_call_target="tpu_custom_call" | custom-call | flops 4000000000 | bytes 15000000 | tf_op jit(solution)/shard_map/ffn_grads/pallas_call | solution.py:569
  159.7 16.1 %layer_rows.7 = bf16[1024,768]{1,0:T(8,128)(2,1)} custom-call(s32[1]{0:T(128)} %constant.7.clone.1.which, f32[768]{0:T(1024)} %bq_ref.9, f32[768]{0:T(1024)} %bo_ref.9, f32[768]{0:T(1024)} %g1_ref.11, f32[768]{0:T(1024)} %s1_ref.9, f32[3072]{0:T(1024)} %bi_ref.9, f32[768]{0:T(1024)} %bb_ref.9, f32[768]{0:T(1024)} %g2_ref.9, ...), custom_call_target="tpu_custom_call", output_to_operand_aliasing={{}: (15, {})} | custom-call | flops 3000000000 | bytes 20000000 | tf_op jit(solution)/shard_map/layer_rows/pallas_call | solution.py:479
  177.1 1.8 collective-permute-start.6
  180.7 5.7 %collective-permute-done.10 = bf16[1536,384]{1,0:T(8,128)(2,1)S(1)} collective-permute-done((bf16[1536,384]{1,0:T(8,128)(2,1)}, bf16[1536,384]{1,0:T(8,128)(2,1)S(1)}, u32[]{:S(2)}, u32[]{:S(2)}) %collective-permute-start.10) | collective-permute-done | bytes 1179680 | tf_op jit(solution)/shard_map/ppermute | solution.py:652
  188.3 18.1 %collective-permute-done.6 = bf16[384,1536]{1,0:T(8,128)(2,1)S(1)} collective-permute-done((bf16[384,1536]{1,0:T(8,128)(2,1)}, bf16[384,1536]{1,0:T(8,128)(2,1)S(1)}, u32[]{:S(2)}, u32[]{:S(2)}) %collective-permute-start.6) | collective-permute-done | bytes 1179680 | tf_op jit(solution)/shard_map/ppermute | solution.py:652
  208.4 4.3 %collective-permute-done.3 = bf16[96,1536]{1,0:T(8,128)(2,1)S(1)} collective-permute-done((bf16[96,1536]{1,0:T(8,128)(2,1)S(1)}, bf16[96,1536]{1,0:T(8,128)(2,1)S(1)}, u32[]{:S(2)}, u32[]{:S(2)}) %collective-permute-start.3) | collective-permute-done | bytes 294944 | tf_op jit(solution)/shard_map/ppermute | solution.py:652
  212.7 2.8 %collective-permute-start.4 = (bf16[48,1536]{1,0:T(8,128)(2,1)S(1)}, bf16[48,1536]{1,0:T(8,128)(2,1)S(1)}, u32[]{:S(2)}, u32[]{:S(2)}) collective-permute-start(bf16[48,1536]{1,0:T(8,128)(2,1)S(1)} %add_convert_fusion.18), channel_id=1, source_target_pairs={{0,16},{2,18},{4,20},{6,22},{8,24},{10,26},{12,28},{14,30},{16,0},... | collective-permute-start | bytes 442376 | tf_op jit(solution)/shard_map/ppermute | solution.py:652
  215.5 7.7 %collective-permute-done.11 = bf16[768,384]{1,0:T(8,128)(2,1)S(1)} collective-permute-done((bf16[768,384]{1,0:T(8,128)(2,1)S(1)}, bf16[768,384]{1,0:T(8,128)(2,1)S(1)}, u32[]{:S(2)}, u32[]{:S(2)}) %collective-permute-start.11) | collective-permute-done | bytes 589856 | tf_op jit(solution)/shard_map/ppermute | solution.py:652
  227.1 7.9 %collective-permute-done.12 = bf16[384,384]{1,0:T(8,128)(2,1)S(1)} collective-permute-done((bf16[384,384]{1,0:T(8,128)(2,1)S(1)}, bf16[384,384]{1,0:T(8,128)(2,1)S(1)}, u32[]{:S(2)}, u32[]{:S(2)}) %collective-permute-start.12) | collective-permute-done | bytes 294944 | tf_op jit(solution)/shard_map/ppermute | solution.py:652
  236.6 1.8 collective-permute-done.8
  238.4 2.7 %collective-permute-start.9 = (bf16[48,1536]{1,0:T(8,128)(2,1)S(1)}, bf16[48,1536]{1,0:T(8,128)(2,1)S(1)}, u32[]{:S(2)}, u32[]{:S(2)}) collective-permute-start(bf16[48,1536]{1,0:T(8,128)(2,1)S(1)} %add_convert_fusion.16), channel_id=1, source_target_pairs={{0,16},{2,18},{4,20},{6,22},{8,24},{10,26},{12,28},{14,30},{16,0},... | collective-permute-start | bytes 442376 | tf_op jit(solution)/shard_map/ppermute | solution.py:652
  241.1 5.9 %collective-permute-done.13 = bf16[192,384]{1,0:T(8,128)(2,1)S(1)} collective-permute-done((bf16[192,384]{1,0:T(8,128)(2,1)S(1)}, bf16[192,384]{1,0:T(8,128)(2,1)S(1)}, u32[]{:S(2)}, u32[]{:S(2)}) %collective-permute-start.13) | collective-permute-done | bytes 147488 | tf_op jit(solution)/shard_map/ppermute | solution.py:652
  (57 shorter events, 18.8 us)
Async XLA Ops:
  7.2 168.6 %all-gather.2.cloned.1.call-start = ((), (), s32[]{:S(2)}) async-start(), calls=%async_computation | async-start | bytes 1216512 | tf_op jit(solution)/shard_map/all_gather | solution.py:707
  61.9 12.5 %copy-start.8 = (f32[1,3840]{1,0:T(1,128)S(1)}, f32[1,3840]{1,0:T(1,128)}, u32[]{:S(2)}) copy-start(f32[1,3840]{1,0:T(1,128)} %get-tuple-element.58) | copy-start | bytes 46084
  61.9 12.6 %copy-start.7 = (f32[1,5376]{1,0:T(1,128)S(1)}, f32[1,5376]{1,0:T(1,128)}, u32[]{:S(2)}) copy-start(f32[1,5376]{1,0:T(1,128)} %get-tuple-element.57) | copy-start | bytes 64516
  73.8 33.7 %collective-permute-start = (bf16[768,1536]{1,0:T(8,128)(2,1)}, bf16[768,1536]{1,0:T(8,128)(2,1)}, u32[]{:S(2)}, u32[]{:S(2)}) collective-permute-start(bf16[768,1536]{1,0:T(8,128)(2,1)} %get-tuple-element.56), channel_id=1, source_target_pairs={{0,1},{1,0},{2,3},{3,2},{4,5},{5,4},{6,7},{7,6},{8,9},{9,8},{10,11... | collective-permute-start | bytes 7077896 | tf_op jit(solution)/shard_map/ppermute | solution.py:692
  74.3 72.8 %collective-permute-start.5 = (bf16[384,5760]{1,0:T(8,128)(2,1)}, bf16[384,5760]{1,0:T(8,128)(2,1)}, u32[]{:S(2)}, u32[]{:S(2)}) collective-permute-start(bf16[384,5760]{1,0:T(8,128)(2,1)} %get-tuple-element.62), channel_id=1, source_target_pairs={{0,1},{1,0},{2,3},{3,2},{4,5},{5,4},{6,7},{7,6},{8,9},{9,8},{10,11... | collective-permute-start | bytes 13271048 | tf_op jit(solution)/shard_map/ppermute | solution.py:688
  91.3 16.3 %copy-start.2 = (bf16[768,1536]{1,0:T(8,128)(2,1)S(1)}, bf16[768,1536]{1,0:T(8,128)(2,1)}, u32[]{:S(2)}) copy-start(bf16[768,1536]{1,0:T(8,128)(2,1)} %get-tuple-element.55) | copy-start | bytes 7077892
  111.2 19.3 %copy-start = (bf16[768,2304]{1,0:T(8,128)(2,1)S(1)}, bf16[768,2304]{1,0:T(8,128)(2,1)}, u32[]{:S(2)}) copy-start(bf16[768,2304]{1,0:T(8,128)(2,1)} %wqkv_h.11) | copy-start | bytes 10616836
  111.2 32.7 %collective-permute-start.1 = (bf16[384,1536]{1,0:T(8,128)(2,1)}, bf16[384,1536]{1,0:T(8,128)(2,1)}, u32[]{:S(2)}, u32[]{:S(2)}) collective-permute-start(bf16[384,1536]{1,0:T(8,128)(2,1)} %get-tuple-element.68), channel_id=1, source_target_pairs={{0,8},{2,10},{4,12},{6,14},{8,0},{10,2},{12,4},{14,6},{16,24},{18,... | collective-permute-start | bytes 3538952 | tf_op jit(solution)/shard_map/ppermute | solution.py:652
  130.5 4.7 %copy-start.5 = (bf16[384,1024]{1,0:T(8,128)(2,1)S(1)}, bf16[384,1024]{1,0:T(8,128)(2,1)}, u32[]{:S(2)}) copy-start(bf16[384,1024]{1,0:T(8,128)(2,1)} %get-tuple-element.42) | copy-start | bytes 2359300
  130.5 4.7 %copy-start.6 = (bf16[384,768]{1,0:T(8,128)(2,1)S(1)}, bf16[384,768]{1,0:T(8,128)(2,1)}, u32[]{:S(2)}) copy-start(bf16[384,768]{1,0:T(8,128)(2,1)} %get-tuple-element.50) | copy-start | bytes 1769476
  135.2 8.7 %copy-start.1 = (bf16[384,1536]{1,0:T(8,128)(2,1)S(1)}, bf16[384,1536]{1,0:T(8,128)(2,1)}, u32[]{:S(2)}) copy-start(bf16[384,1536]{1,0:T(8,128)(2,1)} %get-tuple-element.67) | copy-start | bytes 3538948
  145.4 34.8 %collective-permute-start.2 = (bf16[192,1536]{1,0:T(8,128)(2,1)S(1)}, bf16[192,1536]{1,0:T(8,128)(2,1)S(1)}, u32[]{:S(2)}, u32[]{:S(2)}) collective-permute-start(bf16[192,1536]{1,0:T(8,128)(2,1)S(1)} %get-tuple-element.74), channel_id=1, source_target_pairs={{0,2},{2,0},{4,6},{6,4},{8,10},{10,8},{12,14},{14,12},{16,18},{18,... | collective-permute-start | bytes 1769480 | tf_op jit(solution)/shard_map/ppermute | solution.py:652
  159.3 27.1 %collective-permute-start.10 = (bf16[1536,384]{1,0:T(8,128)(2,1)}, bf16[1536,384]{1,0:T(8,128)(2,1)S(1)}, u32[]{:S(2)}, u32[]{:S(2)}) collective-permute-start(bf16[1536,384]{1,0:T(8,128)(2,1)} %get-tuple-element.66), channel_id=1, source_target_pairs={{0,2},{2,0},{4,6},{6,4},{8,10},{10,8},{12,14},{14,12},{16,18},{18,... | collective-permute-start | bytes 3538952 | tf_op jit(solution)/shard_map/ppermute | solution.py:652
  177.1 9.2 %copy-start.4 = (bf16[1536,384]{1,0:T(8,128)(2,1)S(1)}, bf16[1536,384]{1,0:T(8,128)(2,1)}, u32[]{:S(2)}) copy-start(bf16[1536,384]{1,0:T(8,128)(2,1)} %get-tuple-element.65) | copy-start | bytes 3538948
  177.1 29.2 %collective-permute-start.6 = (bf16[384,1536]{1,0:T(8,128)(2,1)}, bf16[384,1536]{1,0:T(8,128)(2,1)S(1)}, u32[]{:S(2)}, u32[]{:S(2)}) collective-permute-start(bf16[384,1536]{1,0:T(8,128)(2,1)} %get-tuple-element.64), channel_id=1, source_target_pairs={{0,4},{2,6},{4,0},{6,2},{8,12},{10,14},{12,8},{14,10},{16,20},{18,... | collective-permute-start | bytes 3538952 | tf_op jit(solution)/shard_map/ppermute | solution.py:652
  180.3 32.3 %collective-permute-start.3 = (bf16[96,1536]{1,0:T(8,128)(2,1)S(1)}, bf16[96,1536]{1,0:T(8,128)(2,1)S(1)}, u32[]{:S(2)}, u32[]{:S(2)}) collective-permute-start(bf16[96,1536]{1,0:T(8,128)(2,1)S(1)} %get-tuple-element.80), channel_id=1, source_target_pairs={{0,4},{2,6},{4,0},{6,2},{8,12},{10,14},{12,8},{14,10},{16,20},{18,... | collective-permute-start | bytes 884744 | tf_op jit(solution)/shard_map/ppermute | solution.py:652
  186.4 20.0 %copy-start.3 = (bf16[384,1536]{1,0:T(8,128)(2,1)S(1)}, bf16[384,1536]{1,0:T(8,128)(2,1)}, u32[]{:S(2)}) copy-start(bf16[384,1536]{1,0:T(8,128)(2,1)} %get-tuple-element.63) | copy-start | bytes 3538948
  186.7 36.6 %collective-permute-start.11 = (bf16[768,384]{1,0:T(8,128)(2,1)S(1)}, bf16[768,384]{1,0:T(8,128)(2,1)S(1)}, u32[]{:S(2)}, u32[]{:S(2)}) collective-permute-start(bf16[768,384]{1,0:T(8,128)(2,1)S(1)} %get-tuple-element.70), channel_id=1, source_target_pairs={{0,4},{2,6},{4,0},{6,2},{8,12},{10,14},{12,8},{14,10},{16,20},{18,... | collective-permute-start | bytes 1769480 | tf_op jit(solution)/shard_map/ppermute | solution.py:652
  206.6 18.3 %collective-permute-start.7 = (bf16[192,1536]{1,0:T(8,128)(2,1)S(1)}, bf16[192,1536]{1,0:T(8,128)(2,1)S(1)}, u32[]{:S(2)}, u32[]{:S(2)}) collective-permute-start(bf16[192,1536]{1,0:T(8,128)(2,1)S(1)} %get-tuple-element.72), channel_id=1, source_target_pairs={{0,2},{2,0},{4,6},{6,4},{8,10},{10,8},{12,14},{14,12},{16,18},{18,... | collective-permute-start | bytes 1769480 | tf_op jit(solution)/shard_map/ppermute | solution.py:652
  212.7 13.0 %collective-permute-start.4 = (bf16[48,1536]{1,0:T(8,128)(2,1)S(1)}, bf16[48,1536]{1,0:T(8,128)(2,1)S(1)}, u32[]{:S(2)}, u32[]{:S(2)}) collective-permute-start(bf16[48,1536]{1,0:T(8,128)(2,1)S(1)} %add_convert_fusion.18), channel_id=1, source_target_pairs={{0,16},{2,18},{4,20},{6,22},{8,24},{10,26},{12,28},{14,30},{16,0},... | collective-permute-start | bytes 442376 | tf_op jit(solution)/shard_map/ppermute | solution.py:652
  223.4 11.6 %collective-permute-start.12 = (bf16[384,384]{1,0:T(8,128)(2,1)S(1)}, bf16[384,384]{1,0:T(8,128)(2,1)S(1)}, u32[]{:S(2)}, u32[]{:S(2)}) collective-permute-start(bf16[384,384]{1,0:T(8,128)(2,1)S(1)} %get-tuple-element.76), channel_id=1, source_target_pairs={{0,8},{2,10},{4,12},{6,14},{8,0},{10,2},{12,4},{14,6},{16,24},{18,... | collective-permute-start | bytes 884744 | tf_op jit(solution)/shard_map/ppermute | solution.py:652
  225.1 13.3 %collective-permute-start.8 = (bf16[96,1536]{1,0:T(8,128)(2,1)S(1)}, bf16[96,1536]{1,0:T(8,128)(2,1)S(1)}, u32[]{:S(2)}, u32[]{:S(2)}) collective-permute-start(bf16[96,1536]{1,0:T(8,128)(2,1)S(1)} %get-tuple-element.78), channel_id=1, source_target_pairs={{0,8},{2,10},{4,12},{6,14},{8,0},{10,2},{12,4},{14,6},{16,24},{18,... | collective-permute-start | bytes 884744 | tf_op jit(solution)/shard_map/ppermute | solution.py:652
  235.1 12.0 %collective-permute-start.13 = (bf16[192,384]{1,0:T(8,128)(2,1)S(1)}, bf16[192,384]{1,0:T(8,128)(2,1)S(1)}, u32[]{:S(2)}, u32[]{:S(2)}) collective-permute-start(bf16[192,384]{1,0:T(8,128)(2,1)S(1)} %add_convert_fusion.14), channel_id=1, source_target_pairs={{0,16},{2,18},{4,20},{6,22},{8,24},{10,26},{12,28},{14,30},{16,0},... | collective-permute-start | bytes 442376 | tf_op jit(solution)/shard_map/ppermute | solution.py:652
  238.4 10.2 %collective-permute-start.9 = (bf16[48,1536]{1,0:T(8,128)(2,1)S(1)}, bf16[48,1536]{1,0:T(8,128)(2,1)S(1)}, u32[]{:S(2)}, u32[]{:S(2)}) collective-permute-start(bf16[48,1536]{1,0:T(8,128)(2,1)S(1)} %add_convert_fusion.16), channel_id=1, source_target_pairs={{0,16},{2,18},{4,20},{6,22},{8,24},{10,26},{12,28},{14,30},{16,0},... | collective-permute-start | bytes 442376 | tf_op jit(solution)/shard_map/ppermute | solution.py:652
Sparse Core Ops, SparseCore 0:
  75.3 57.1 all-gather.1
